TPU v7x, 512 devices: a whole 4x8x8 slice. The times are simulated.
512 devices in a mesh: dp: 8 (over z), expert: 64 (over x, y, core).
Axes of the slice: x: 4, y: 8, z: 8, core: 2. Of those that a mesh axis runs over, the one named last changes fastest.
Arguments:
- tokens: bfloat16 [65536, 1024], P(('dp', 'expert')), may hold values from -6 to 6
- cotangent: bfloat16 [65536, 1024], P(('dp', 'expert')), may hold values from -6 to 6
- routes: int32 [65536, 8], P(('dp', 'expert')), may hold values from 0 to 63, as said below
- combine: float32 [65536, 8], P(('dp', 'expert')), may hold values from 0.1 to 0.5
- w_gate: bfloat16 [64, 1024, 384], P('expert', 'dp'), may hold values from -0.1875 to 0.1875
- w_up: bfloat16 [64, 1024, 384], P('expert', 'dp'), may hold values from -0.1875 to 0.1875
- w_down: bfloat16 [64, 384, 1024], P('expert', None, 'dp'), may hold values from -0.3125 to 0.3125
Outputs:
- mixed: bfloat16 [65536, 1024], P(('dp', 'expert'))
- input_grad: bfloat16 [65536, 1024], P(('dp', 'expert'))
- combine_grad: float32 [65536, 8], P(('dp', 'expert'))
Inputs may be any that keep to these rules, and one draw needn't show every extreme that they name: `routes`: each row names 8 different experts. Among the rows of one device (aligned blocks of 128 rows) each of 2 frequent experts, the same ones on every device, is named by 48 to 56 rows, and every other expert by at most 15 rows, with the counts of the other experts on one device differing by at most one. In every draw some device has a frequent expert named by exactly 56 rows and some device an other expert named by exactly 15 rows.
All inputs are finite; a program needn't handle non-finite values.
Results may differ from a plain program's by a relative error of at most 0.017.
Values may be sent and summed in bfloat16 or wider, within the bound.
No kernel may reach another device: no remote copies, remote signals or barrier semaphores. Data moves between devices by JAX's collectives and lax.ppermute only.
A program may use at most 128 MiB of HBM per device.

v0:
```python
import jax
import jax.numpy as jnp
from jax import lax
from jax.sharding import PartitionSpec as P

HOT = 2


def broadcast(block, axis, owner):
    block = jnp.where(lax.axis_index(axis) == owner, block, jnp.zeros_like(block))
    return lax.psum(block, axis)


def to_owner(array, owners, local_count):
    shape = array.shape
    grouped = array.reshape((owners, local_count) + shape[1:])
    grouped = jnp.swapaxes(grouped, 0, 1)
    return grouped.reshape((local_count, owners * shape[1]) + shape[2:])


def from_owner(array, owners, local_count):
    shape = array.shape
    grouped = array.reshape((local_count, owners, shape[1] // owners) + shape[2:])
    grouped = jnp.swapaxes(grouped, 0, 1)
    return grouped.reshape((owners * local_count, shape[1] // owners) + shape[2:])


def expert_block(row_x, row_dy, row_g, w_g, w_u, w_d):
    gate_pre = jnp.einsum("erd,edf->erf", row_x, w_g, preferred_element_type=jnp.float32)
    up_proj = jnp.einsum("erd,edf->erf", row_x, w_u, preferred_element_type=jnp.float32)
    sigmoid_val = jax.nn.sigmoid(gate_pre)
    silu_val = gate_pre * sigmoid_val
    hidden = (silu_val * up_proj).astype(jnp.bfloat16)
    expert_out = jnp.einsum("erf,efd->erd", hidden, w_d, preferred_element_type=jnp.float32).astype(
        jnp.bfloat16
    )
    dot_grad = jnp.einsum("erd,efd->erf", row_dy, w_d, preferred_element_type=jnp.float32)
    hidden_grad = row_g[:, :, None] * dot_grad
    gate_grad = (
        hidden_grad * up_proj * sigmoid_val * (1.0 + gate_pre * (1.0 - sigmoid_val))
    ).astype(jnp.bfloat16)
    up_grad = (hidden_grad * silu_val).astype(jnp.bfloat16)
    row_grad = jnp.einsum("erf,edf->erd", gate_grad, w_g, preferred_element_type=jnp.float32)
    row_grad = (
        row_grad + jnp.einsum("erf,edf->erd", up_grad, w_u, preferred_element_type=jnp.float32)
    ).astype(jnp.bfloat16)
    return (expert_out, row_grad)


def on_device(tokens, cotangent, routes, combine, w_gate, w_up, w_down):
    tok_rows, width = tokens.shape
    topk = routes.shape[1]
    owners = lax.axis_size("expert")
    local_count = w_gate.shape[0]
    experts = local_count * owners
    pairs = tok_rows * topk
    hot_most = min(tok_rows, 7 * pairs // (2 * experts))
    hot_least = min(tok_rows * 3 // 4, 3 * pairs // experts)
    capacity = (pairs - HOT * hot_least + experts - HOT - 1) // (experts - HOT)
    cold_rows = experts * capacity
    pool_rows = cold_rows + HOT * hot_most
    expert_ids = routes.reshape(-1)
    one_hot = (expert_ids[:, None] == jnp.arange(experts, dtype=jnp.int32)[None, :]).astype(
        jnp.int32
    )
    rank_in = jnp.sum((jnp.cumsum(one_hot, axis=0) - 1) * one_hot, axis=1)
    counts = jnp.sum(one_hot, axis=0)
    top_counts, top_ids = lax.top_k(counts, HOT)
    hot_list = jnp.sort(top_ids)
    match = expert_ids[:, None] == hot_list[None, :]
    is_hot = jnp.any(match, axis=1)
    hot_rank = (
        jnp.sum(jnp.where(match, jnp.arange(HOT, dtype=jnp.int32)[None, :] * hot_most, 0), axis=1)
        + rank_in
    )
    slot_index = jnp.where(is_hot, cold_rows + hot_rank, expert_ids * capacity + rank_in)
    token_index = jnp.arange(pairs, dtype=jnp.int32) // topk
    source_token = jnp.full((pool_rows,), tok_rows, jnp.int32).at[slot_index].set(token_index)
    source_pair = (
        jnp.full((pool_rows,), pairs, jnp.int32)
        .at[slot_index]
        .set(jnp.arange(pairs, dtype=jnp.int32))
    )
    pool_x = jnp.take(tokens, source_token, axis=0, mode="fill", fill_value=0)
    pool_dy = jnp.take(cotangent, source_token, axis=0, mode="fill", fill_value=0)
    pool_g = jnp.take(combine.reshape(-1), source_pair, axis=0, mode="fill", fill_value=0)
    send_x = pool_x[:cold_rows].reshape(experts, capacity, width)
    send_dy = pool_dy[:cold_rows].reshape(experts, capacity, width)
    send_g = pool_g[:cold_rows].reshape(experts, capacity)
    hot_x = pool_x[cold_rows:].reshape(HOT, hot_most, width)
    hot_dy = pool_dy[cold_rows:].reshape(HOT, hot_most, width)
    hot_g = pool_g[cold_rows:].reshape(HOT, hot_most)
    recv_x, recv_dy, recv_g = (
        lax.all_to_all(send_x, "expert", split_axis=0, concat_axis=0, tiled=True),
        lax.all_to_all(send_dy, "expert", split_axis=0, concat_axis=0, tiled=True),
        lax.all_to_all(
            send_g.astype(jnp.bfloat16), "expert", split_axis=0, concat_axis=0, tiled=True
        ).astype(send_g.dtype),
    )
    full_gate, full_up, full_down = (
        lax.all_gather(w_gate, "dp", axis=1, tiled=True),
        lax.all_gather(w_up, "dp", axis=1, tiled=True),
        lax.all_gather(w_down, "dp", axis=2, tiled=True),
    )
    gate_list = []
    up_list = []
    down_list = []
    for which in range(HOT):
        root = hot_list[which] // local_count
        local_slot = hot_list[which] % local_count
        piece_gate = lax.dynamic_index_in_dim(w_gate, local_slot, 0, keepdims=False)
        piece_up = lax.dynamic_index_in_dim(w_up, local_slot, 0, keepdims=False)
        piece_down = lax.dynamic_index_in_dim(w_down, local_slot, 0, keepdims=False)
        shard_gate, shard_up, shard_down = (
            broadcast(piece_gate, "expert", root),
            broadcast(piece_up, "expert", root),
            broadcast(piece_down, "expert", root),
        )
        got_gate, got_up, got_down = (
            lax.all_gather(shard_gate, "dp", axis=0, tiled=True),
            lax.all_gather(shard_up, "dp", axis=0, tiled=True),
            lax.all_gather(shard_down, "dp", axis=1, tiled=True),
        )
        gate_list.append(got_gate)
        up_list.append(got_up)
        down_list.append(got_down)
    hot_out, hot_grad = expert_block(
        hot_x, hot_dy, hot_g, jnp.stack(gate_list), jnp.stack(up_list), jnp.stack(down_list)
    )
    row_x = to_owner(recv_x, owners, local_count)
    row_dy = to_owner(recv_dy, owners, local_count)
    row_g = to_owner(recv_g, owners, local_count)
    expert_out, row_grad = expert_block(row_x, row_dy, row_g, full_gate, full_up, full_down)
    back_out, back_grad = (
        lax.all_to_all(
            from_owner(expert_out, owners, local_count),
            "expert",
            split_axis=0,
            concat_axis=0,
            tiled=True,
        ),
        lax.all_to_all(
            from_owner(row_grad, owners, local_count),
            "expert",
            split_axis=0,
            concat_axis=0,
            tiled=True,
        ),
    )
    pool_out = jnp.concatenate(
        [back_out.reshape(cold_rows, width), hot_out.reshape(HOT * hot_most, width)], axis=0
    )
    pool_grad = jnp.concatenate(
        [back_grad.reshape(cold_rows, width), hot_grad.reshape(HOT * hot_most, width)], axis=0
    )
    out_pairs = pool_out[slot_index].reshape(tok_rows, topk, width)
    grad_pairs = pool_grad[slot_index].reshape(tok_rows, topk, width)
    mixed = jnp.einsum("tk,tkd->td", combine, out_pairs.astype(jnp.float32)).astype(jnp.bfloat16)
    input_grad = jnp.sum(grad_pairs.astype(jnp.float32), axis=1).astype(jnp.bfloat16)
    combine_grad = jnp.einsum(
        "tkd,td->tk", out_pairs, cotangent, preferred_element_type=jnp.float32
    )
    return (mixed, input_grad, combine_grad)


def solution(mesh):
    placed = (
        P(("dp", "expert"), None),
        P(("dp", "expert"), None),
        P(("dp", "expert"), None),
        P(("dp", "expert"), None),
        P("expert", "dp", None),
        P("expert", "dp", None),
        P("expert", None, "dp"),
    )
    return jax.shard_map(
        on_device,
        mesh=mesh,
        in_specs=placed,
        out_specs=(P(("dp", "expert"), None), P(("dp", "expert"), None), P(("dp", "expert"), None)),
        check_vma=False,
    )
```

profile of v0, /device:TPU:22, one launch (start us, length us, event | category | flops | bytes accessed | tf_op | source)
XLA Modules:
  0.0 678.3 jit_solution(17495965251228169367)
XLA Ops:
  10.0 18.0 %reduce-window.6 = s32[64,8,128]{2,1,0:T(8,128)S(1)} reduce-window(s32[64,8,128]{2,1,0:T(8,128)S(1)} %fusion.22, s32[]{:T(128)} %constant.105.clone.1), window={size=1x1x128 pad=0_0x0_0x127_0}, to_apply=%region_5.6 | reduce-window | flops 8323072 | bytes 524292 | tf_op jit(solution)/shard_map/reduce-window
  31.9 4.3 scatter_custom_fusion.1
  36.2 4.4 gather_fusion.1
  41.4 10.6 %all-to-all-start.2 = ((bf16[64,1,15]{2,1,0:T(2,128)(2,1)}), bf16[64,1,15]{2,1,0:T(2,128)(2,1)S(1)}, u32[]{:S(2)}, u32[]{:S(2)}) async-start(bf16[64,1,15]{2,1,0:T(2,128)(2,1)} %convert_element_type.86), calls=%async_computation.2 | async-start | bytes 65536 | tf_op jit(solution)/shard_map/all_to_all | solution.py:96
  52.0 4.3 scatter_custom_fusion
  56.4 4.4 gather_fusion.4
  60.8 4.9 gather_fusion.3
  65.7 3.3 broadcast_select_fusion
  72.9 10.6 %all-to-all-start = ((bf16[64,15,1024]{2,1,0:T(8,128)(2,1)}), bf16[64,15,1024]{2,1,0:T(8,128)(2,1)}, u32[]{:S(2)}, u32[]{:S(2)}) async-start(bf16[64,15,1024]{2,1,0:T(8,128)(2,1)} %reshape.219), calls=%async_computation | async-start | bytes 4194304 | tf_op jit(solution)/shard_map/all_to_all | solution.py:94
  85.0 3.7 reshape.229
  88.7 43.9 %all-to-all-done = bf16[64,15,1024]{2,1,0:T(8,128)(2,1)} async-done(((bf16[64,15,1024]{2,1,0:T(8,128)(2,1)}), bf16[64,15,1024]{2,1,0:T(8,128)(2,1)}, u32[]{:S(2)}, u32[]{:S(2)}) %all-to-all-start) | async-done | bytes 1966112 | tf_op jit(solution)/shard_map/all_to_all | solution.py:94
  132.7 8.0 %all-to-all-start.3 = ((bf16[64,15,1024]{2,1,0:T(8,128)(2,1)}), bf16[64,15,1024]{2,1,0:T(8,128)(2,1)}, u32[]{:S(2)}, u32[]{:S(2)}) async-start(bf16[64,15,1024]{2,1,0:T(8,128)(2,1)} %reshape.229), calls=%async_computation.3 | async-start | bytes 4194304 | tf_op jit(solution)/shard_map/all_to_all | solution.py:95
  140.7 34.4 %all_gather.27 = bf16[1,1024,384]{2,1,0:T(8,128)(2,1)} all-gather(bf16[1,128,384]{2,1,0:T(8,128)(2,1)S(1)} %copy-done.11), channel_id=1, replica_groups=mesh['dp'=8,'expert'=64] {'dp'}, dimensions={1}, use_global_device_ids=true | all-gather | bytes 884736 | tf_op jit(solution)/shard_map/all_gather | solution.py:101
  175.2 26.3 %all_gather.28 = bf16[1,1024,384]{2,1,0:T(8,128)(2,1)S(1)} all-gather(bf16[1,128,384]{2,1,0:T(8,128)(2,1)S(1)} %copy-done.9), channel_id=1, replica_groups=mesh['dp'=8,'expert'=64] {'dp'}, dimensions={1}, use_global_device_ids=true | all-gather | bytes 884736 | tf_op jit(solution)/shard_map/all_gather | solution.py:102
  201.5 27.0 %all_gather.29 = bf16[1,384,1024]{2,1,0:T(8,128)(2,1)} all-gather(bf16[1,384,128]{2,1,0:T(8,128)(2,1)S(1)} %copy-done.10), channel_id=1, replica_groups=mesh['dp'=8,'expert'=64] {'dp'}, dimensions={2}, use_global_device_ids=true | all-gather | bytes 884736 | tf_op jit(solution)/shard_map/all_gather | solution.py:103
  228.5 3.7 reshape.220
  232.2 3.0 fusion.16
  240.2 3.8 reshape_transpose_reshape.8
  244.0 10.4 %all-to-all-start.1 = ((bf16[64,15,1024]{2,1,0:T(8,128)(2,1)}), bf16[64,15,1024]{2,1,0:T(8,128)(2,1)}, u32[]{:S(2)}, u32[]{:S(2)}) async-start(bf16[64,15,1024]{2,1,0:T(8,128)(2,1)} %reshape_transpose_reshape.8), calls=%async_computation.1 | async-start | bytes 4194304 | tf_op jit(solution)/shard_map/all_to_all | solution.py:135
  262.7 193.6 %all-reduce.3.cloned.1.call-done = (bf16[384,128]{1,0:T(8,128)(2,1)}, bf16[384,128]{1,0:T(8,128)(2,1)}, bf16[128,384]{1,0:T(8,128)(2,1)}, bf16[128,384]{1,0:T(8,...) async-done(((bf16[384,128]{1,0:T(8,128)(2,1)}, bf16[384,128]{1,0:T(8,128)(2,1)}, bf16[128,384]{1,0:T(8,128)(2,1)}, bf16[128,384]{1,0:T(8,128)(2,1)}, ...) | async-done | bytes 589840 | tf_op jit(solution)/shard_map/psum | solution.py:11
  456.2 30.5 %all_gather.31 = bf16[1024,384]{1,0:T(8,128)(2,1)} all-gather(bf16[128,384]{1,0:T(8,128)(2,1)} %get-tuple-element.17), channel_id=1, replica_groups=mesh['dp'=8,'expert'=64] {'dp'}, dimensions={0}, use_global_device_ids=true | all-gather | bytes 884736 | tf_op jit(solution)/shard_map/all_gather | solution.py:120
  496.3 11.2 %all-to-all-start.4 = ((bf16[64,15,1024]{2,1,0:T(8,128)(2,1)}), bf16[64,15,1024]{2,1,0:T(8,128)(2,1)}, u32[]{:S(2)}, u32[]{:S(2)}) async-start(bf16[64,15,1024]{2,1,0:T(8,128)(2,1)} %reshape_transpose_reshape.9), calls=%async_computation.4 | async-start | bytes 4194304 | tf_op jit(solution)/shard_map/all_to_all | solution.py:142
  507.5 26.3 %all_gather.30 = bf16[1024,384]{1,0:T(8,128)(2,1)S(1)} all-gather(bf16[128,384]{1,0:T(8,128)(2,1)S(1)} %copy-done.17), channel_id=1, replica_groups=mesh['dp'=8,'expert'=64] {'dp'}, dimensions={0}, use_global_device_ids=true | all-gather | bytes 884736 | tf_op jit(solution)/shard_map/all_gather | solution.py:120
  534.2 26.2 %all_gather.33 = bf16[1024,384]{1,0:T(8,128)(2,1)S(1)} all-gather(bf16[128,384]{1,0:T(8,128)(2,1)S(1)} %copy-done.16), channel_id=1, replica_groups=mesh['dp'=8,'expert'=64] {'dp'}, dimensions={0}, use_global_device_ids=true | all-gather | bytes 884736 | tf_op jit(solution)/shard_map/all_gather | solution.py:121
  560.4 26.4 %all_gather.32 = bf16[1024,384]{1,0:T(8,128)(2,1)S(1)} all-gather(bf16[128,384]{1,0:T(8,128)(2,1)S(1)} %copy-done.15), channel_id=1, replica_groups=mesh['dp'=8,'expert'=64] {'dp'}, dimensions={0}, use_global_device_ids=true | all-gather | bytes 884736 | tf_op jit(solution)/shard_map/all_gather | solution.py:121
  587.3 26.7 %all_gather.35 = bf16[384,1024]{1,0:T(8,128)(2,1)S(1)} all-gather(bf16[384,128]{1,0:T(8,128)(2,1)S(1)} %copy-done.14), channel_id=1, replica_groups=mesh['dp'=8,'expert'=64] {'dp'}, dimensions={1}, use_global_device_ids=true | all-gather | bytes 884736 | tf_op jit(solution)/shard_map/all_gather | solution.py:122
  614.0 24.3 %all_gather.34 = bf16[384,1024]{1,0:T(8,128)(2,1)S(1)} all-gather(bf16[384,128]{1,0:T(8,128)(2,1)S(1)} %copy-done.13), channel_id=1, replica_groups=mesh['dp'=8,'expert'=64] {'dp'}, dimensions={1}, use_global_device_ids=true | all-gather | bytes 884736 | tf_op jit(solution)/shard_map/all_gather | solution.py:122
  640.8 3.8 reshape.224
  646.3 5.4 gather_fusion
  656.9 3.7 reshape.231
  662.4 5.4 gather_fusion.2
  667.8 3.7 bitcast_reduce_fusion
  (122 shorter events, 46.0 us)
Async XLA Ops:
  7.2 49.2 %copy-start = (bf16[128,1024]{1,0:T(8,128)(2,1)S(1)}, bf16[128,1024]{1,0:T(8,128)(2,1)}, u32[]{:S(2)}) copy-start(bf16[128,1024]{1,0:T(8,128)(2,1)} %param.10) | copy-start | bytes 786436
  31.4 0.5 copy-start.19
  41.4 30.9 %all-to-all-start.2 = ((bf16[64,1,15]{2,1,0:T(2,128)(2,1)}), bf16[64,1,15]{2,1,0:T(2,128)(2,1)S(1)}, u32[]{:S(2)}, u32[]{:S(2)}) async-start(bf16[64,1,15]{2,1,0:T(2,128)(2,1)} %convert_element_type.86), calls=%async_computation.2 | async-start | bytes 65536 | tf_op jit(solution)/shard_map/all_to_all | solution.py:96
  56.4 4.4 copy-start.1
  69.1 1.4 copy-start.2
  72.3 11.3 %copy-start.3 = (bf16[1072,1024]{1,0:T(8,128)(2,1)S(1)}, bf16[1072,1024]{1,0:T(8,128)(2,1)}, u32[]{:S(2)}) copy-start(bf16[1072,1024]{1,0:T(8,128)(2,1)} %get-tuple-element.25) | copy-start | bytes 6586372
  72.3 0.6 copy-start.12
  72.9 59.8 %all-to-all-start = ((bf16[64,15,1024]{2,1,0:T(8,128)(2,1)}), bf16[64,15,1024]{2,1,0:T(8,128)(2,1)}, u32[]{:S(2)}, u32[]{:S(2)}) async-start(bf16[64,15,1024]{2,1,0:T(8,128)(2,1)} %reshape.219), calls=%async_computation | async-start | bytes 4194304 | tf_op jit(solution)/shard_map/all_to_all | solution.py:94
  88.7 52.0 %copy-start.11 = (bf16[1,128,384]{2,1,0:T(8,128)(2,1)S(1)}, bf16[1,128,384]{2,1,0:T(8,128)(2,1)}, u32[]{:S(2)}) copy-start(bf16[1,128,384]{2,1,0:T(8,128)(2,1)} %param.13) | copy-start | bytes 294916
  88.7 86.5 %copy-start.9 = (bf16[1,128,384]{2,1,0:T(8,128)(2,1)S(1)}, bf16[1,128,384]{2,1,0:T(8,128)(2,1)}, u32[]{:S(2)}) copy-start(bf16[1,128,384]{2,1,0:T(8,128)(2,1)} %param.14) | copy-start | bytes 294916
  88.7 112.8 %copy-start.10 = (bf16[1,384,128]{2,1,0:T(8,128)(2,1)S(1)}, bf16[1,384,128]{2,1,0:T(8,128)(2,1)}, u32[]{:S(2)}) copy-start(bf16[1,384,128]{2,1,0:T(8,128)(2,1)} %param.15) | copy-start | bytes 294916
  132.7 111.3 %all-to-all-start.3 = ((bf16[64,15,1024]{2,1,0:T(8,128)(2,1)}), bf16[64,15,1024]{2,1,0:T(8,128)(2,1)}, u32[]{:S(2)}, u32[]{:S(2)}) async-start(bf16[64,15,1024]{2,1,0:T(8,128)(2,1)} %reshape.229), calls=%async_computation.3 | async-start | bytes 4194304 | tf_op jit(solution)/shard_map/all_to_all | solution.py:95
  232.2 3.0 copy-start.5
  235.3 1.2 copy-start.20
  235.3 2.4 copy-start.7
  236.5 1.2 copy-start.22
  244.0 252.3 %all-to-all-start.1 = ((bf16[64,15,1024]{2,1,0:T(8,128)(2,1)}), bf16[64,15,1024]{2,1,0:T(8,128)(2,1)}, u32[]{:S(2)}, u32[]{:S(2)}) async-start(bf16[64,15,1024]{2,1,0:T(8,128)(2,1)} %reshape_transpose_reshape.8), calls=%async_computation.1 | async-start | bytes 4194304 | tf_op jit(solution)/shard_map/all_to_all | solution.py:135
  254.4 6.4 copy-start.18
  254.4 201.8 %all-reduce.3.cloned.1.call-start = ((), (), s32[]{:S(2)}) async-start(), calls=%async_computation.5 | async-start | bytes 1179648 | tf_op jit(solution)/shard_map/psum | solution.py:11
  489.3 2.5 copy-start.6
  489.4 2.5 copy-start.21
  489.4 2.5 copy-start.23
  496.3 11.3 %copy-start.17 = (bf16[128,384]{1,0:T(8,128)(2,1)S(1)}, bf16[128,384]{1,0:T(8,128)(2,1)}, u32[]{:S(2)}) copy-start(bf16[128,384]{1,0:T(8,128)(2,1)} %get-tuple-element.18) | copy-start | bytes 294916
  496.3 37.6 %copy-start.8 = (bf16[1024,384]{1,0:T(8,128)(2,1)S(1)}, bf16[1024,384]{1,0:T(8,128)(2,1)}, u32[]{:S(2)}) copy-start(bf16[1024,384]{1,0:T(8,128)(2,1)} %all_gather.31) | copy-start | bytes 2359300
  496.3 160.6 %all-to-all-start.4 = ((bf16[64,15,1024]{2,1,0:T(8,128)(2,1)}), bf16[64,15,1024]{2,1,0:T(8,128)(2,1)}, u32[]{:S(2)}, u32[]{:S(2)}) async-start(bf16[64,15,1024]{2,1,0:T(8,128)(2,1)} %reshape_transpose_reshape.9), calls=%async_computation.4 | async-start | bytes 4194304 | tf_op jit(solution)/shard_map/all_to_all | solution.py:142
  507.5 26.7 %copy-start.16 = (bf16[128,384]{1,0:T(8,128)(2,1)S(1)}, bf16[128,384]{1,0:T(8,128)(2,1)}, u32[]{:S(2)}) copy-start(bf16[128,384]{1,0:T(8,128)(2,1)} %get-tuple-element.15) | copy-start | bytes 294916
  533.8 26.6 %copy-start.15 = (bf16[128,384]{1,0:T(8,128)(2,1)S(1)}, bf16[128,384]{1,0:T(8,128)(2,1)}, u32[]{:S(2)}) copy-start(bf16[128,384]{1,0:T(8,128)(2,1)} %get-tuple-element.16) | copy-start | bytes 294916
  560.4 26.9 %copy-start.14 = (bf16[384,128]{1,0:T(8,128)(2,1)S(1)}, bf16[384,128]{1,0:T(8,128)(2,1)}, u32[]{:S(2)}) copy-start(bf16[384,128]{1,0:T(8,128)(2,1)} %get-tuple-element.13) | copy-start | bytes 294916
  586.8 27.1 %copy-start.13 = (bf16[384,128]{1,0:T(8,128)(2,1)S(1)}, bf16[384,128]{1,0:T(8,128)(2,1)}, u32[]{:S(2)}) copy-start(bf16[384,128]{1,0:T(8,128)(2,1)} %get-tuple-element.14) | copy-start | bytes 294916
  651.7 3.2 copy-start.4
Sparse Core Ops, SparseCore 0:
  259.9 196.3 all-reduce.2
where the time goes:
time: 680 us; the launch traced here: 678 us
  blocking collectives  248 us (36%)
  waiting for transfers between devices  238 us (35%)
  local copies, waits for them, and re-layouts  71.4 us (11%)
  starting transfers between devices  51 us (8%)
  other arithmetic  35.4 us (5%)
  matrix products  19 us (3%)
  between operations  15.9 us (2%)
    psum x1, waiting for transfers between devices, broadcast(): return lax.psum(block, axis)  194 us
    all_gather x2, blocking collectives, on_device(): lax.all_gather(shard_gate, 'dp', axis=0, tiled=True)  56.8 us
    all_gather x2, blocking collectives, on_device(): lax.all_gather(shard_up, 'dp', axis=0, tiled=True)  52.6 us
    all_gather x2, blocking collectives, on_device(): lax.all_gather(shard_down, 'dp', axis=1, tiled=True)  51 us
    all_to_all x1, waiting for transfers between devices, on_device(): lax.all_to_all(send_x, 'expert', split_axis=0, concat_axis=0, tiled=True)  43.9 us
    all_gather x1, blocking collectives, on_device(): lax.all_gather(w_gate, 'dp', axis=1, tiled=True)  34.4 us
    all_gather x1, blocking collectives, on_device(): lax.all_gather(w_down, 'dp', axis=2, tiled=True)  27 us
    all_gather x1, blocking collectives, on_device(): lax.all_gather(w_up, 'dp', axis=1, tiled=True)  26.3 us
  transfers between devices with their start and end apart: 6, of which 2 were waited for; matrix products, arithmetic and copies ran while one was open for 11% of the time, Pallas kernels for 0%

commit v1 on v0

--- a/solution.py
+++ b/solution.py
@@ -4,6 +4,27 @@
 from jax.sharding import PartitionSpec as P
 
 HOT = 2
+
+
+def gather_around(array, axis, dim):
+    size, index, rows = (lax.axis_size(axis), lax.axis_index(axis), array.shape[dim])
+    ahead = [(i, (i + 1) % size) for i in range(size)]
+    backward = [(i, (i - 1) % size) for i in range(size)]
+    out = jnp.zeros((*array.shape[:dim], size * rows, *array.shape[dim + 1 :]), array.dtype)
+    out = lax.dynamic_update_slice_in_dim(out, array, index * rows, axis=dim)
+    from_left = from_right = array
+    halfway = size // 2
+    for step in range(1, halfway + 1):
+        from_left = lax.ppermute(from_left, axis, ahead)
+        out = lax.dynamic_update_slice_in_dim(
+            out, from_left, (index - step) % size * rows, axis=dim
+        )
+        if step < size - halfway:
+            from_right = lax.ppermute(from_right, axis, backward)
+            out = lax.dynamic_update_slice_in_dim(
+                out, from_right, (index + step) % size * rows, axis=dim
+            )
+    return out
 
 
 def broadcast(block, axis, owner):
@@ -118,7 +139,7 @@
         )
         got_gate, got_up, got_down = (
             lax.all_gather(shard_gate, "dp", axis=0, tiled=True),
-            lax.all_gather(shard_up, "dp", axis=0, tiled=True),
+            gather_around(shard_up, "dp", 0),
             lax.all_gather(shard_down, "dp", axis=1, tiled=True),
         )
         gate_list.append(got_gate)

time: 680 us -> 632 us (0.929)
  the two profiles are of different devices: /device:TPU:22 before, /device:TPU:1 now
where the time goes in v1:
time: 632 us; the launch traced here: 630 us
  waiting for transfers between devices  190 us (30%)
  blocking collectives  161 us (25%)
  starting transfers between devices  114 us (18%)
  local copies, waits for them, and re-layouts  92.1 us (15%)
  other arithmetic  34.7 us (5%)
  matrix products  23 us (4%)
  between operations  16.2 us (3%)
    psum x1, waiting for transfers between devices, broadcast(): return lax.psum(block, axis)  131 us
    all_to_all x1, waiting for transfers between devices, on_device(): lax.all_to_all(send_x, 'expert', split_axis=0, concat_axis=0, tiled=True)  43.3 us
    all_gather x2, blocking collectives, on_device(): lax.all_gather(shard_down, 'dp', axis=1, tiled=True)  42.6 us
    all_gather x2, blocking collectives, on_device(): lax.all_gather(shard_gate, 'dp', axis=0, tiled=True)  42.4 us
    all_gather x1, blocking collectives, on_device(): lax.all_gather(w_gate, 'dp', axis=1, tiled=True)  30 us
    ppermute x6, starting transfers between devices, gather_around(): from_right = lax.ppermute(from_right, axis, backward)  25.5 us
    all_gather x1, blocking collectives, on_device(): lax.all_gather(w_up, 'dp', axis=1, tiled=True)  24.1 us
    all_gather x1, blocking collectives, on_device(): lax.all_gather(w_down, 'dp', axis=2, tiled=True)  21.8 us
  transfers between devices with their start and end apart: 20, of which 3 were waited for; matrix products, arithmetic and copies ran while one was open for 15% of the time, Pallas kernels for 0%

profile of v1, /device:TPU:1, one launch (start us, length us, event | category | flops | bytes accessed | tf_op | source)
XLA Modules:
  0.0 630.4 jit_solution(13996278403419357662)
XLA Ops:
  10.0 18.0 %reduce-window.6 = s32[64,8,128]{2,1,0:T(8,128)S(1)} reduce-window(s32[64,8,128]{2,1,0:T(8,128)S(1)} %fusion.22, s32[]{:T(128)} %constant.179.clone.1), window={size=1x1x128 pad=0_0x0_0x127_0}, to_apply=%region_5.6 | reduce-window | flops 8323072 | bytes 524292 | tf_op jit(solution)/shard_map/reduce-window
  31.6 4.3 scatter_custom_fusion.1
  35.9 4.4 gather_fusion.1
  41.1 11.6 %all-to-all-start.2 = ((bf16[64,1,15]{2,1,0:T(2,128)(2,1)}), bf16[64,1,15]{2,1,0:T(2,128)(2,1)S(1)}, u32[]{:S(2)}, u32[]{:S(2)}) async-start(bf16[64,1,15]{2,1,0:T(2,128)(2,1)} %convert_element_type.86), calls=%async_computation.2 | async-start | bytes 65536 | tf_op jit(solution)/shard_map/all_to_all | solution.py:117
  52.7 4.3 scatter_custom_fusion
  57.1 4.4 gather_fusion.4
  61.5 4.9 gather_fusion.3
  73.0 10.6 %all-to-all-start = ((bf16[64,15,1024]{2,1,0:T(8,128)(2,1)}), bf16[64,15,1024]{2,1,0:T(8,128)(2,1)}, u32[]{:S(2)}, u32[]{:S(2)}) async-start(bf16[64,15,1024]{2,1,0:T(8,128)(2,1)} %reshape.251), calls=%async_computation | async-start | bytes 4194304 | tf_op jit(solution)/shard_map/all_to_all | solution.py:115
  87.0 3.8 reshape.261
  91.5 43.3 %all-to-all-done = bf16[64,15,1024]{2,1,0:T(8,128)(2,1)} async-done(((bf16[64,15,1024]{2,1,0:T(8,128)(2,1)}), bf16[64,15,1024]{2,1,0:T(8,128)(2,1)}, u32[]{:S(2)}, u32[]{:S(2)}) %all-to-all-start) | async-done | bytes 1966112 | tf_op jit(solution)/shard_map/all_to_all | solution.py:115
  134.8 6.0 all-to-all-start.3
  144.4 30.0 %all_gather.21 = bf16[1,1024,384]{2,1,0:T(8,128)(2,1)} all-gather(bf16[1,128,384]{2,1,0:T(8,128)(2,1)S(1)} %copy-done.15), channel_id=1, replica_groups=mesh['dp'=8,'expert'=64] {'dp'}, dimensions={1}, use_global_device_ids=true | all-gather | bytes 884736 | tf_op jit(solution)/shard_map/all_gather | solution.py:122
  174.4 24.1 %all_gather.22 = bf16[1,1024,384]{2,1,0:T(8,128)(2,1)} all-gather(bf16[1,128,384]{2,1,0:T(8,128)(2,1)S(1)} %copy-done.16), channel_id=1, replica_groups=mesh['dp'=8,'expert'=64] {'dp'}, dimensions={1}, use_global_device_ids=true | all-gather | bytes 884736 | tf_op jit(solution)/shard_map/all_gather | solution.py:123
  198.5 21.8 %all_gather.23 = bf16[1,384,1024]{2,1,0:T(8,128)(2,1)} all-gather(bf16[1,384,128]{2,1,0:T(8,128)(2,1)S(1)} %copy-done.17), channel_id=1, replica_groups=mesh['dp'=8,'expert'=64] {'dp'}, dimensions={2}, use_global_device_ids=true | all-gather | bytes 884736 | tf_op jit(solution)/shard_map/all_gather | solution.py:124
  220.6 131.1 %all-reduce.3.cloned.1.call-done = (bf16[384,128]{1,0:T(8,128)(2,1)}, bf16[384,128]{1,0:T(8,128)(2,1)}, bf16[128,384]{1,0:T(8,128)(2,1)}, bf16[128,384]{1,0:T(8,...) async-done(((bf16[384,128]{1,0:T(8,128)(2,1)}, bf16[384,128]{1,0:T(8,128)(2,1)}, bf16[128,384]{1,0:T(8,128)(2,1)}, bf16[128,384]{1,0:T(8,128)(2,1)}, ...) | async-done | bytes 589840 | tf_op jit(solution)/shard_map/psum | solution.py:32
  351.7 5.6 collective-permute-start.8
  359.2 4.6 collective-permute-start.1
  365.8 20.9 %all_gather.25 = bf16[1024,384]{1,0:T(8,128)(2,1)S(1)} all-gather(bf16[128,384]{1,0:T(8,128)(2,1)} %get-tuple-element.17), channel_id=1, replica_groups=mesh['dp'=8,'expert'=64] {'dp'}, dimensions={0}, use_global_device_ids=true | all-gather | bytes 884736 | tf_op jit(solution)/shard_map/all_gather | solution.py:141
  386.7 21.5 %all_gather.24 = bf16[1024,384]{1,0:T(8,128)(2,1)S(1)} all-gather(bf16[128,384]{1,0:T(8,128)(2,1)} %get-tuple-element.18), channel_id=1, replica_groups=mesh['dp'=8,'expert'=64] {'dp'}, dimensions={0}, use_global_device_ids=true | all-gather | bytes 884736 | tf_op jit(solution)/shard_map/all_gather | solution.py:141
  420.5 21.4 %all-to-all-start.1 = ((bf16[64,15,1024]{2,1,0:T(8,128)(2,1)}), bf16[64,15,1024]{2,1,0:T(8,128)(2,1)S(1)}, u32[]{:S(2)}, u32[]{:S(2)}) async-start(bf16[64,15,1024]{2,1,0:T(8,128)(2,1)} %reshape_transpose_reshape.8), calls=%async_computation.1 | async-start | bytes 4194304 | tf_op jit(solution)/shard_map/all_to_all | solution.py:156
  444.4 21.5 %all_gather.27 = bf16[384,1024]{1,0:T(8,128)(2,1)S(1)} all-gather(bf16[384,128]{1,0:T(8,128)(2,1)} %get-tuple-element.13), channel_id=1, replica_groups=mesh['dp'=8,'expert'=64] {'dp'}, dimensions={1}, use_global_device_ids=true | all-gather | bytes 884736 | tf_op jit(solution)/shard_map/all_gather | solution.py:143
  465.9 21.1 %all_gather.26 = bf16[384,1024]{1,0:T(8,128)(2,1)S(1)} all-gather(bf16[384,128]{1,0:T(8,128)(2,1)S(1)} %copy-done.19), channel_id=1, replica_groups=mesh['dp'=8,'expert'=64] {'dp'}, dimensions={1}, use_global_device_ids=true | all-gather | bytes 884736 | tf_op jit(solution)/shard_map/all_gather | solution.py:143
  495.2 3.7 collective-permute-start.3
  507.1 4.5 collective-permute-start.12
  513.6 4.6 collective-permute-start.5
  521.6 3.8 reshape.262
  532.6 3.7 reshape_transpose_reshape.9
  536.3 21.4 %all-to-all-start.4 = ((bf16[64,15,1024]{2,1,0:T(8,128)(2,1)}), bf16[64,15,1024]{2,1,0:T(8,128)(2,1)}, u32[]{:S(2)}, u32[]{:S(2)}) async-start(bf16[64,15,1024]{2,1,0:T(8,128)(2,1)} %reshape_transpose_reshape.9), calls=%async_computation.4 | async-start | bytes 4194304 | tf_op jit(solution)/shard_map/all_to_all | solution.py:163
  582.9 5.4 gather_fusion
  593.5 15.4 %all-to-all-done.4 = bf16[64,15,1024]{2,1,0:T(8,128)(2,1)} async-done(((bf16[64,15,1024]{2,1,0:T(8,128)(2,1)}), bf16[64,15,1024]{2,1,0:T(8,128)(2,1)}, u32[]{:S(2)}, u32[]{:S(2)}) %all-to-all-start.4) | async-done | bytes 1966112 | tf_op jit(solution)/shard_map/all_to_all | solution.py:163
  608.9 3.8 reshape.263
  614.4 5.4 gather_fusion.2
  (174 shorter events, 103.2 us)
Async XLA Ops:
  7.2 49.9 %copy-start = (bf16[128,1024]{1,0:T(8,128)(2,1)S(1)}, bf16[128,1024]{1,0:T(8,128)(2,1)}, u32[]{:S(2)}) copy-start(bf16[128,1024]{1,0:T(8,128)(2,1)} %param.10) | copy-start | bytes 786436
  41.1 31.9 %all-to-all-start.2 = ((bf16[64,1,15]{2,1,0:T(2,128)(2,1)}), bf16[64,1,15]{2,1,0:T(2,128)(2,1)S(1)}, u32[]{:S(2)}, u32[]{:S(2)}) async-start(bf16[64,1,15]{2,1,0:T(2,128)(2,1)} %convert_element_type.86), calls=%async_computation.2 | async-start | bytes 65536 | tf_op jit(solution)/shard_map/all_to_all | solution.py:117
  57.1 4.4 copy-start.1
  73.0 12.5 %copy-start.3 = (bf16[1072,1024]{1,0:T(8,128)(2,1)S(1)}, bf16[1072,1024]{1,0:T(8,128)(2,1)}, u32[]{:S(2)}) copy-start(bf16[1072,1024]{1,0:T(8,128)(2,1)} %get-tuple-element.25) | copy-start | bytes 6586372
  73.0 61.8 %all-to-all-start = ((bf16[64,15,1024]{2,1,0:T(8,128)(2,1)}), bf16[64,15,1024]{2,1,0:T(8,128)(2,1)}, u32[]{:S(2)}, u32[]{:S(2)}) async-start(bf16[64,15,1024]{2,1,0:T(8,128)(2,1)} %reshape.251), calls=%async_computation | async-start | bytes 4194304 | tf_op jit(solution)/shard_map/all_to_all | solution.py:115
  91.5 49.4 %copy-start.17 = (bf16[1,384,128]{2,1,0:T(8,128)(2,1)S(1)}, bf16[1,384,128]{2,1,0:T(8,128)(2,1)}, u32[]{:S(2)}) copy-start(bf16[1,384,128]{2,1,0:T(8,128)(2,1)} %param.15) | copy-start | bytes 294916
  91.5 50.1 %copy-start.15 = (bf16[1,128,384]{2,1,0:T(8,128)(2,1)S(1)}, bf16[1,128,384]{2,1,0:T(8,128)(2,1)}, u32[]{:S(2)}) copy-start(bf16[1,128,384]{2,1,0:T(8,128)(2,1)} %param.13) | copy-start | bytes 294916
  134.8 285.7 %all-to-all-start.3 = ((bf16[64,15,1024]{2,1,0:T(8,128)(2,1)}), bf16[64,15,1024]{2,1,0:T(8,128)(2,1)}, u32[]{:S(2)}, u32[]{:S(2)}) async-start(bf16[64,15,1024]{2,1,0:T(8,128)(2,1)} %reshape.261), calls=%async_computation.3 | async-start | bytes 4194304 | tf_op jit(solution)/shard_map/all_to_all | solution.py:116
  140.9 210.9 %all-reduce.3.cloned.1.call-start = ((), (), s32[]{:S(2)}) async-start(), calls=%async_computation.5 | async-start | bytes 1179648 | tf_op jit(solution)/shard_map/psum | solution.py:32
  351.7 138.2 %collective-permute-start.8 = (bf16[128,384]{1,0:T(8,128)(2,1)}, bf16[128,384]{1,0:T(8,128)(2,1)}, u32[]{:S(2)}, u32[]{:S(2)}) collective-permute-start(bf16[128,384]{1,0:T(8,128)(2,1)} %get-tuple-element.15), channel_id=1, source_target_pairs={{0,448},{64,0},{128,64},{192,128},{256,192},{320,256},{384,320},{4... | collective-permute-start | bytes 294920 | tf_op jit(solution)/shard_map/ppermute | solution.py:23
  357.3 135.1 %collective-permute-start.7 = (bf16[128,384]{1,0:T(8,128)(2,1)}, bf16[128,384]{1,0:T(8,128)(2,1)}, u32[]{:S(2)}, u32[]{:S(2)}) collective-permute-start(bf16[128,384]{1,0:T(8,128)(2,1)} %get-tuple-element.15), channel_id=1, source_target_pairs={{0,64},{64,128},{128,192},{192,256},{256,320},{320,384},{384,448},... | collective-permute-start | bytes 294920 | tf_op jit(solution)/shard_map/ppermute | solution.py:18
  359.2 136.0 %collective-permute-start.1 = (bf16[128,384]{1,0:T(8,128)(2,1)}, bf16[128,384]{1,0:T(8,128)(2,1)}, u32[]{:S(2)}, u32[]{:S(2)}) collective-permute-start(bf16[128,384]{1,0:T(8,128)(2,1)} %get-tuple-element.16), channel_id=1, source_target_pairs={{0,448},{64,0},{128,64},{192,128},{256,192},{320,256},{384,320},{4... | collective-permute-start | bytes 294920 | tf_op jit(solution)/shard_map/ppermute | solution.py:23
  363.8 135.1 %collective-permute-start = (bf16[128,384]{1,0:T(8,128)(2,1)}, bf16[128,384]{1,0:T(8,128)(2,1)}, u32[]{:S(2)}, u32[]{:S(2)}) collective-permute-start(bf16[128,384]{1,0:T(8,128)(2,1)} %get-tuple-element.16), channel_id=1, source_target_pairs={{0,64},{64,128},{128,192},{192,256},{256,320},{320,384},{384,448},... | collective-permute-start | bytes 294920 | tf_op jit(solution)/shard_map/ppermute | solution.py:18
  420.5 45.4 %copy-start.19 = (bf16[384,128]{1,0:T(8,128)(2,1)S(1)}, bf16[384,128]{1,0:T(8,128)(2,1)}, u32[]{:S(2)}) copy-start(bf16[384,128]{1,0:T(8,128)(2,1)} %get-tuple-element.14) | copy-start | bytes 294916
  420.5 115.8 %all-to-all-start.1 = ((bf16[64,15,1024]{2,1,0:T(8,128)(2,1)}), bf16[64,15,1024]{2,1,0:T(8,128)(2,1)S(1)}, u32[]{:S(2)}, u32[]{:S(2)}) async-start(bf16[64,15,1024]{2,1,0:T(8,128)(2,1)} %reshape_transpose_reshape.8), calls=%async_computation.1 | async-start | bytes 4194304 | tf_op jit(solution)/shard_map/all_to_all | solution.py:156
  441.9 45.2 %copy-start.18 = (bf16[112,1024]{1,0:T(8,128)(2,1)S(1)}, bf16[112,1024]{1,0:T(8,128)(2,1)}, u32[]{:S(2)}) copy-start(bf16[112,1024]{1,0:T(8,128)(2,1)} %slice.62) | copy-start | bytes 688132
  465.9 23.3 %copy-start.7 = (bf16[384,1024]{1,0:T(8,128)(2,1)}, bf16[384,1024]{1,0:T(8,128)(2,1)S(1)}, u32[]{:S(2)}) copy-start(bf16[384,1024]{1,0:T(8,128)(2,1)S(1)} %all_gather.27) | copy-start | bytes 2359300
  487.0 15.4 %copy-start.9 = (bf16[384,1024]{1,0:T(8,128)(2,1)}, bf16[384,1024]{1,0:T(8,128)(2,1)S(1)}, u32[]{:S(2)}) copy-start(bf16[384,1024]{1,0:T(8,128)(2,1)S(1)} %all_gather.26) | copy-start | bytes 2359300
  489.9 17.2 %collective-permute-start.10 = (bf16[128,384]{1,0:T(8,128)(2,1)}, bf16[128,384]{1,0:T(8,128)(2,1)S(1)}, u32[]{:S(2)}, u32[]{:S(2)}) collective-permute-start(bf16[128,384]{1,0:T(8,128)(2,1)} %collective-permute-done.8), channel_id=1, source_target_pairs={{0,448},{64,0},{128,64},{192,128},{256,192},{320,256},{384,320},{4... | collective-permute-start | bytes 294920 | tf_op jit(solution)/shard_map/ppermute | solution.py:23
  492.4 19.2 %collective-permute-start.9 = (bf16[128,384]{1,0:T(8,128)(2,1)}, bf16[128,384]{1,0:T(8,128)(2,1)}, u32[]{:S(2)}, u32[]{:S(2)}) collective-permute-start(bf16[128,384]{1,0:T(8,128)(2,1)} %collective-permute-done.7), channel_id=1, source_target_pairs={{0,64},{64,128},{128,192},{192,256},{256,320},{320,384},{384,448},... | collective-permute-start | bytes 294920 | tf_op jit(solution)/shard_map/ppermute | solution.py:18
  495.2 18.3 %collective-permute-start.3 = (bf16[128,384]{1,0:T(8,128)(2,1)}, bf16[128,384]{1,0:T(8,128)(2,1)}, u32[]{:S(2)}, u32[]{:S(2)}) collective-permute-start(bf16[128,384]{1,0:T(8,128)(2,1)} %collective-permute-done.1), channel_id=1, source_target_pairs={{0,448},{64,0},{128,64},{192,128},{256,192},{320,256},{384,320},{4... | collective-permute-start | bytes 294920 | tf_op jit(solution)/shard_map/ppermute | solution.py:23
  499.0 19.2 %collective-permute-start.2 = (bf16[128,384]{1,0:T(8,128)(2,1)}, bf16[128,384]{1,0:T(8,128)(2,1)}, u32[]{:S(2)}, u32[]{:S(2)}) collective-permute-start(bf16[128,384]{1,0:T(8,128)(2,1)} %collective-permute-done), channel_id=1, source_target_pairs={{0,64},{64,128},{128,192},{192,256},{256,320},{320,384},{384,448},... | collective-permute-start | bytes 294920 | tf_op jit(solution)/shard_map/ppermute | solution.py:18
  507.1 62.1 %collective-permute-start.12 = (bf16[128,384]{1,0:T(8,128)(2,1)S(1)}, bf16[128,384]{1,0:T(8,128)(2,1)}, u32[]{:S(2)}, u32[]{:S(2)}) collective-permute-start(bf16[128,384]{1,0:T(8,128)(2,1)S(1)} %collective-permute-done.10), channel_id=1, source_target_pairs={{0,448},{64,0},{128,64},{192,128},{256,192},{320,256},{384,320},{4... | collective-permute-start | bytes 294920 | tf_op jit(solution)/shard_map/ppermute | solution.py:23
  511.6 49.8 %collective-permute-start.11 = (bf16[128,384]{1,0:T(8,128)(2,1)}, bf16[128,384]{1,0:T(8,128)(2,1)}, u32[]{:S(2)}, u32[]{:S(2)}) collective-permute-start(bf16[128,384]{1,0:T(8,128)(2,1)} %collective-permute-done.9), channel_id=1, source_target_pairs={{0,64},{64,128},{128,192},{192,256},{256,320},{320,384},{384,448},... | collective-permute-start | bytes 294920 | tf_op jit(solution)/shard_map/ppermute | solution.py:18
  513.6 57.2 %collective-permute-start.5 = (bf16[128,384]{1,0:T(8,128)(2,1)}, bf16[128,384]{1,0:T(8,128)(2,1)}, u32[]{:S(2)}, u32[]{:S(2)}) collective-permute-start(bf16[128,384]{1,0:T(8,128)(2,1)} %collective-permute-done.3), channel_id=1, source_target_pairs={{0,448},{64,0},{128,64},{192,128},{256,192},{320,256},{384,320},{4... | collective-permute-start | bytes 294920 | tf_op jit(solution)/shard_map/ppermute | solution.py:23
  518.2 45.4 %collective-permute-start.4 = (bf16[128,384]{1,0:T(8,128)(2,1)}, bf16[128,384]{1,0:T(8,128)(2,1)}, u32[]{:S(2)}, u32[]{:S(2)}) collective-permute-start(bf16[128,384]{1,0:T(8,128)(2,1)} %collective-permute-done.2), channel_id=1, source_target_pairs={{0,64},{64,128},{128,192},{192,256},{256,320},{320,384},{384,448},... | collective-permute-start | bytes 294920 | tf_op jit(solution)/shard_map/ppermute | solution.py:18
  536.3 72.6 %all-to-all-start.4 = ((bf16[64,15,1024]{2,1,0:T(8,128)(2,1)}), bf16[64,15,1024]{2,1,0:T(8,128)(2,1)}, u32[]{:S(2)}, u32[]{:S(2)}) async-start(bf16[64,15,1024]{2,1,0:T(8,128)(2,1)} %reshape_transpose_reshape.9), calls=%async_computation.4 | async-start | bytes 4194304 | tf_op jit(solution)/shard_map/all_to_all | solution.py:163
  561.5 14.0 %copy-start.8 = (bf16[384,1024]{1,0:T(8,128)(2,1)S(1)}, bf16[384,1024]{1,0:T(8,128)(2,1)}, u32[]{:S(2)}) copy-start(bf16[384,1024]{1,0:T(8,128)(2,1)} %copy-done.7) | copy-start | bytes 2359300
  561.5 14.0 %copy-start.10 = (bf16[384,1024]{1,0:T(8,128)(2,1)S(1)}, bf16[384,1024]{1,0:T(8,128)(2,1)}, u32[]{:S(2)}) copy-start(bf16[384,1024]{1,0:T(8,128)(2,1)} %copy-done.9) | copy-start | bytes 2359300
  561.5 14.0 %copy-start.26 = (f32[2,56,384]{2,1,0:T(8,128)S(1)}, f32[2,56,384]{2,1,0:T(8,128)}, u32[]{:S(2)}) copy-start(f32[2,56,384]{2,1,0:T(8,128)} %fusion.8) | copy-start | bytes 516100
  561.5 10.9 %collective-permute-start.13 = (bf16[128,384]{1,0:T(8,128)(2,1)}, bf16[128,384]{1,0:T(8,128)(2,1)S(1)}, u32[]{:S(2)}, u32[]{:S(2)}) collective-permute-start(bf16[128,384]{1,0:T(8,128)(2,1)} %collective-permute-done.11), channel_id=1, source_target_pairs={{0,64},{64,128},{128,192},{192,256},{256,320},{320,384},{384,448},... | collective-permute-start | bytes 294920 | tf_op jit(solution)/shard_map/ppermute | solution.py:18
  563.5 9.5 %collective-permute-start.6 = (bf16[128,384]{1,0:T(8,128)(2,1)}, bf16[128,384]{1,0:T(8,128)(2,1)S(1)}, u32[]{:S(2)}, u32[]{:S(2)}) collective-permute-start(bf16[128,384]{1,0:T(8,128)(2,1)} %collective-permute-done.4), channel_id=1, source_target_pairs={{0,64},{64,128},{128,192},{192,256},{256,320},{320,384},{384,448},... | collective-permute-start | bytes 294920 | tf_op jit(solution)/shard_map/ppermute | solution.py:18
  (16 other events, 35.1 us)
Sparse Core Ops, SparseCore 0:
  146.3 205.3 all-reduce.2
